TPU v7x, 128 devices: a whole 4x4x4 slice. The times are simulated.
128 devices in a mesh: chain: 128 (over z, y, x, core).
Axes of the slice: x: 4, y: 4, z: 4, core: 2. Of those that a mesh axis runs over, the one named last changes fastest.
Arguments:
- sections: float32 [128, 2, 4, 2, 128, 128], P('chain'), may hold values from -1.2 to 1.2
- probes: float32 [2, 2, 128, 16384], P(None, None, None, 'chain'), may hold values from -6 to 6
Outputs:
- prefixes: float32 [128, 2, 4, 2, 128, 128], P('chain')
- reflected: float32 [2, 2, 128, 16384], P(None, None, None, 'chain')
- transmitted: float32 [2, 2, 128, 16384], P(None, None, None, 'chain')
All inputs are finite; a program needn't handle non-finite values.
Results may differ from a plain program's by a relative error of at most 0.0003.
Values sent between devices are 32-bit elements; how exact they have to be, the bound alone decides.
No kernel may reach another device: no remote copies, remote signals or barrier semaphores. Data moves between devices by JAX's collectives and lax.ppermute only.
A program may use at most 128 MiB of HBM per device.

v0:
```python
import jax
import jax.numpy as jnp
from jax import lax
from jax.sharding import PartitionSpec as P

INV_STEPS = 9


precise = lax.Precision.HIGHEST


def shifted(block, axis, distance):
    devices = range(lax.axis_size(axis))
    route = [(i - distance, i) for i in devices if i - distance in devices]
    return lax.ppermute(block, axis, route)


def broadcast(value, axis, source):
    kept = jnp.where(lax.axis_index(axis) == source, value, 0).astype(value.dtype)
    return lax.psum(kept, axis)


def complex_product(former, latter):
    former_re = former[..., 0, :, :]
    former_im = former[..., 1, :, :]
    latter_re = latter[..., 0, :, :]
    latter_im = latter[..., 1, :, :]
    real_part = jnp.einsum(
        "...ij,...jk->...ik", former_re, latter_re, precision=precise
    ) - jnp.einsum("...ij,...jk->...ik", former_im, latter_im, precision=precise)
    imag_part = jnp.einsum(
        "...ij,...jk->...ik", former_re, latter_im, precision=precise
    ) + jnp.einsum("...ij,...jk->...ik", former_im, latter_re, precision=precise)
    return jnp.stack([real_part, imag_part], axis=-3)


def unit_like(block):
    vacant = jnp.zeros_like(block[..., 0, :, :])
    diagonal_one = vacant + jnp.eye(block.shape[-1], dtype=block.dtype)
    return jnp.stack([diagonal_one, vacant], axis=-3)


def scattering_identity(matrix):
    unit_block = unit_like(matrix[:, 0])
    vacant = jnp.zeros_like(unit_block)
    return jnp.stack([vacant, unit_block, unit_block, vacant], axis=1)


def redheffer(first, second):
    first_left, first_back, first_fore, first_right = (
        first[:, 0],
        first[:, 1],
        first[:, 2],
        first[:, 3],
    )
    second_left, second_back, second_fore, second_right = (
        second[:, 0],
        second[:, 1],
        second[:, 2],
        second[:, 3],
    )
    unit_block = unit_like(first_left)
    bounce = complex_product(second_left, first_right)
    system = unit_block - bounce
    resolvent = unit_block
    for iteration in range(INV_STEPS):
        resolvent = complex_product(
            resolvent, 2.0 * unit_block - complex_product(system, resolvent)
        )
    leading = complex_product(first_back, resolvent)
    new_left = first_left + complex_product(leading, complex_product(second_left, first_fore))
    new_back = complex_product(leading, second_back)
    trailing = second_fore + complex_product(
        complex_product(second_fore, first_right), complex_product(resolvent, second_left)
    )
    new_fore = complex_product(trailing, first_fore)
    new_right = second_right + complex_product(trailing, complex_product(first_right, second_back))
    return jnp.stack([new_left, new_back, new_fore, new_right], axis=1)


def local(sections, probes):
    device_count = lax.axis_size("chain")
    position = lax.axis_index("chain")
    running = [sections[0]]
    aggregate = running[-1]
    identity_matrix = scattering_identity(aggregate)
    inclusive = aggregate
    for stride_bit in range((device_count - 1).bit_length()):
        stride = 1 << stride_bit
        earlier = shifted(inclusive, "chain", stride)
        inclusive = jnp.where(position >= stride, redheffer(earlier, inclusive), inclusive)
    before = shifted(inclusive, "chain", 1)
    before = jnp.where(position >= 1, before, identity_matrix)
    prefixes = jnp.stack([redheffer(before, section_prefix) for section_prefix in running], axis=0)
    chain_total = broadcast(inclusive, "chain", device_count - 1)
    reflected = complex_product(chain_total[:, 0], probes)
    transmitted = complex_product(chain_total[:, 2], probes)
    return (prefixes, reflected, transmitted)


def solution(mesh):
    placed = (P("chain", None, None, None, None, None), P(None, None, None, "chain"))
    return jax.shard_map(
        local,
        mesh=mesh,
        in_specs=placed,
        out_specs=(
            P("chain", None, None, None, None, None),
            P(None, None, None, "chain"),
            P(None, None, None, "chain"),
        ),
        check_vma=False,
    )
```

profile of v0, /device:TPU:1, one launch (start us, length us, event | category | flops | bytes accessed | tf_op | source)
XLA Modules:
  0.0 654.7 jit_solution(490692437851682438)
XLA Ops:
  7.2 1.3 copy.92
  8.5 4.5 collective-permute-start
  13.2 11.6 %collective-permute-done = f32[2,4,2,128,128]{4,3,0,2,1:T(8,128)} collective-permute-done((f32[2,4,2,128,128]{4,3,0,2,1:T(8,128)S(1)}, f32[2,4,2,128,128]{4,3,0,2,1:T(8,128)}, u32[]{:S(2)}, u32[]{:S(2)}) %collective-permute-start) | collective-permute-done | bytes 1048608 | tf_op jit(solution)/shard_map/ppermute | solution.py:15
  24.8 1.2 slice_bitcast_fusion.44
  60.2 9.5 %fusion.294 = f32[2,1,1,128,128]{4,3,0,2,1:T(8,128)S(1)} fusion(f32[2,128,128]{2,1,0:T(8,128)S(1)} %fusion.866, f32[2,128,128]{2,1,0:T(8,128)S(1)} %convolution_add_fusion.214, f32[2,128,128]{2,1,0:T(8,128)S(1)} %convolution_subtract_fusion.213), kind=kOutput, calls=%fused_computation.729 | convolution fusion | flops 50364416 | bytes 524288 | tf_op jit(solution)/shard_map/...ij,...jk->...ik/dot_general | solution.py:33
  69.8 1.2 slice_add_fusion.13
  71.2 1.1 maximum_select_fusion
  72.3 4.1 collective-permute-start.1
  76.4 1.2 slice_bitcast_fusion.39
  77.5 19.1 %collective-permute-done.1 = f32[2,4,2,128,128]{4,3,0,2,1:T(8,128)} collective-permute-done((f32[2,4,2,128,128]{4,3,0,2,1:T(8,128)}, f32[2,4,2,128,128]{4,3,0,2,1:T(8,128)}, u32[]{:S(2)}, u32[]{:S(2)}) %collective-permute-start.1) | collective-permute-done | bytes 1048608 | tf_op jit(solution)/shard_map/ppermute | solution.py:15
  96.7 1.2 slice_bitcast_fusion.40
  133.4 1.2 maximum_select_fusion.1
  134.6 6.4 collective-permute-start.2
  141.0 1.2 slice_bitcast_fusion.33
  142.2 17.5 %collective-permute-done.2 = f32[2,4,2,128,128]{4,3,0,2,1:T(8,128)} collective-permute-done((f32[2,4,2,128,128]{4,3,0,2,1:T(8,128)}, f32[2,4,2,128,128]{4,3,0,2,1:T(8,128)}, u32[]{:S(2)}, u32[]{:S(2)}) %collective-permute-start.2) | collective-permute-done | bytes 1048608 | tf_op jit(solution)/shard_map/ppermute | solution.py:15
  159.7 1.2 slice_bitcast_fusion.34
  194.3 1.2 slice_add_fusion.9
  196.7 1.3 maximum_select_fusion.2
  198.0 5.0 collective-permute-start.3
  203.0 1.2 slice_bitcast_fusion.27
  204.2 15.0 %collective-permute-done.3 = f32[2,4,2,128,128]{4,3,0,2,1:T(8,128)} collective-permute-done((f32[2,4,2,128,128]{4,3,0,2,1:T(8,128)}, f32[2,4,2,128,128]{4,3,0,2,1:T(8,128)}, u32[]{:S(2)}, u32[]{:S(2)}) %collective-permute-start.3) | collective-permute-done | bytes 1048608 | tf_op jit(solution)/shard_map/ppermute | solution.py:15
  219.1 1.2 slice_bitcast_fusion.28
  254.0 1.2 slice_add_fusion.7
  255.2 1.1 slice_add_fusion.8
  256.5 1.4 maximum_select_fusion.3
  258.0 6.8 %collective-permute-start.4 = (f32[2,4,2,128,128]{4,3,0,2,1:T(8,128)}, f32[2,4,2,128,128]{4,3,0,2,1:T(8,128)}, u32[]{:S(2)}, u32[]{:S(2)}) collective-permute-start(f32[2,4,2,128,128]{4,3,0,2,1:T(8,128)} %maximum_select_fusion.3), channel_id=1, source_target_pairs={{0,16},{1,17},{2,18},{3,19},{4,20},{5,21},{6,22},{7,23},{8,24},{9,... | collective-permute-start | bytes 3145736 | tf_op jit(solution)/shard_map/ppermute | solution.py:15
  264.8 1.2 slice_bitcast_fusion.21
  266.0 14.1 %collective-permute-done.4 = f32[2,4,2,128,128]{4,3,0,2,1:T(8,128)} collective-permute-done((f32[2,4,2,128,128]{4,3,0,2,1:T(8,128)}, f32[2,4,2,128,128]{4,3,0,2,1:T(8,128)}, u32[]{:S(2)}, u32[]{:S(2)}) %collective-permute-start.4) | collective-permute-done | bytes 1048608 | tf_op jit(solution)/shard_map/ppermute | solution.py:15
  280.1 1.2 slice_bitcast_fusion.22
  314.8 1.3 slice_add_fusion.5
  316.1 1.1 slice_add_fusion.6
  317.4 1.6 maximum_select_fusion.4
  319.0 4.9 collective-permute-start.5
  323.9 1.2 slice_bitcast_fusion.15
  325.1 11.2 %collective-permute-done.5 = f32[2,4,2,128,128]{4,3,0,2,1:T(8,128)} collective-permute-done((f32[2,4,2,128,128]{4,3,0,2,1:T(8,128)}, f32[2,4,2,128,128]{4,3,0,2,1:T(8,128)}, u32[]{:S(2)}, u32[]{:S(2)}) %collective-permute-start.5) | collective-permute-done | bytes 1048608 | tf_op jit(solution)/shard_map/ppermute | solution.py:15
  336.3 1.2 slice_bitcast_fusion.16
  371.0 1.3 slice_add_fusion.3
  373.7 1.5 maximum_select_fusion.5
  375.2 7.3 %collective-permute-start.6 = (f32[2,4,2,128,128]{4,3,0,2,1:T(8,128)}, f32[2,4,2,128,128]{4,3,0,2,1:T(8,128)}, u32[]{:S(2)}, u32[]{:S(2)}) collective-permute-start(f32[2,4,2,128,128]{4,3,0,2,1:T(8,128)} %maximum_select_fusion.5), channel_id=1, source_target_pairs={{0,64},{1,65},{2,66},{3,67},{4,68},{5,69},{6,70},{7,71},{8,72},{9,... | collective-permute-start | bytes 3145736 | tf_op jit(solution)/shard_map/ppermute | solution.py:15
  382.5 1.2 slice_bitcast_fusion.9
  383.7 10.5 %collective-permute-done.6 = f32[2,4,2,128,128]{4,3,0,2,1:T(8,128)} collective-permute-done((f32[2,4,2,128,128]{4,3,0,2,1:T(8,128)}, f32[2,4,2,128,128]{4,3,0,2,1:T(8,128)}, u32[]{:S(2)}, u32[]{:S(2)}) %collective-permute-start.6) | collective-permute-done | bytes 1048608 | tf_op jit(solution)/shard_map/ppermute | solution.py:15
  394.2 1.2 slice_bitcast_fusion.10
  429.2 1.1 slice_add_fusion.1
  431.5 1.9 broadcast_select_fusion
  433.5 1.2 copy-done.74
  434.7 22.3 %collective-permute-start.7 = (f32[2,4,2,128,128]{4,3,0,2,1:T(8,128)S(1)}, f32[2,4,2,128,128]{4,3,0,2,1:T(8,128)}, u32[]{:S(2)}, u32[]{:S(2)}) collective-permute-start(f32[2,4,2,128,128]{4,3,0,2,1:T(8,128)S(1)} %copy-done.74), channel_id=1, source_target_pairs={{0,1},{1,2},{2,3},{3,4},{4,5},{5,6},{6,7},{7,8},{8,9},{9,10},{10,1... | collective-permute-start | bytes 3145736 | tf_op jit(solution)/shard_map/ppermute | solution.py:15
  457.0 147.0 %all-reduce.3.cloned.1.call-done = f32[2,4,2,128,128]{4,3,0,2,1:T(8,128)} async-done(((f32[2,4,2,128,128]{4,3,0,2,1:T(8,128)}), f32[2,4,2,128,128]{4,3,0,2,1:T(8,128)}) %all-reduce.3.cloned.1.call-update) | async-done | bytes 1048592 | tf_op jit(solution)/shard_map/psum | solution.py:20
  609.7 1.3 maximum_select_fusion.7
  (1211 shorter events, 276.3 us)
Async XLA Ops:
  7.2 596.8 %all-reduce.3.cloned.1.call-start = ((), (), s32[]{:S(2)}) async-start(), calls=%async_computation | async-start | bytes 2097152 | tf_op jit(solution)/shard_map/psum | solution.py:20
  8.5 42.9 %copy-start.33 = (f32[1,2,4,2,128,128]{5,4,1,3,2,0:T(8,128)}, f32[1,2,4,2,128,128]{5,4,1,3,2,0:T(8,128)S(1)}, u32[]{:S(2)}) copy-start(f32[1,2,4,2,128,128]{5,4,1,3,2,0:T(8,128)S(1)} %copy.92) | copy-start | bytes 3145732
  8.5 16.2 %collective-permute-start = (f32[2,4,2,128,128]{4,3,0,2,1:T(8,128)S(1)}, f32[2,4,2,128,128]{4,3,0,2,1:T(8,128)}, u32[]{:S(2)}, u32[]{:S(2)}) collective-permute-start(f32[2,4,2,128,128]{4,3,0,2,1:T(8,128)S(1)} %bitcast.3017), channel_id=1, source_target_pairs={{0,1},{1,2},{2,3},{3,4},{4,5},{5,6},{6,7},{7,8},{8,9},{9,10},{10,1... | collective-permute-start | bytes 3145736 | tf_op jit(solution)/shard_map/ppermute | solution.py:15
  13.2 36.9 %copy-start.51 = (f32[2,2,128,128]{3,2,0,1:T(8,128)}, f32[2,2,128,128]{3,2,0,1:T(8,128)S(1)}, u32[]{:S(2)}) copy-start(f32[2,2,128,128]{3,2,0,1:T(8,128)S(1)} %get-tuple-element.53) | copy-start | bytes 786436
  72.3 24.4 %collective-permute-start.1 = (f32[2,4,2,128,128]{4,3,0,2,1:T(8,128)}, f32[2,4,2,128,128]{4,3,0,2,1:T(8,128)}, u32[]{:S(2)}, u32[]{:S(2)}) collective-permute-start(f32[2,4,2,128,128]{4,3,0,2,1:T(8,128)} %maximum_select_fusion), channel_id=1, source_target_pairs={{0,2},{1,3},{2,4},{3,5},{4,6},{5,7},{6,8},{7,9},{8,10},{9,11},{10,... | collective-permute-start | bytes 3145736 | tf_op jit(solution)/shard_map/ppermute | solution.py:15
  134.6 25.1 %collective-permute-start.2 = (f32[2,4,2,128,128]{4,3,0,2,1:T(8,128)}, f32[2,4,2,128,128]{4,3,0,2,1:T(8,128)}, u32[]{:S(2)}, u32[]{:S(2)}) collective-permute-start(f32[2,4,2,128,128]{4,3,0,2,1:T(8,128)} %maximum_select_fusion.1), channel_id=1, source_target_pairs={{0,4},{1,5},{2,6},{3,7},{4,8},{5,9},{6,10},{7,11},{8,12},{9,13},{1... | collective-permute-start | bytes 3145736 | tf_op jit(solution)/shard_map/ppermute | solution.py:15
  198.0 21.1 %collective-permute-start.3 = (f32[2,4,2,128,128]{4,3,0,2,1:T(8,128)}, f32[2,4,2,128,128]{4,3,0,2,1:T(8,128)}, u32[]{:S(2)}, u32[]{:S(2)}) collective-permute-start(f32[2,4,2,128,128]{4,3,0,2,1:T(8,128)} %maximum_select_fusion.2), channel_id=1, source_target_pairs={{0,8},{1,9},{2,10},{3,11},{4,12},{5,13},{6,14},{7,15},{8,16},{9,17... | collective-permute-start | bytes 3145736 | tf_op jit(solution)/shard_map/ppermute | solution.py:15
  253.9 2.4 copy-start.35
  254.0 2.4 copy-start.19
  258.0 22.1 %collective-permute-start.4 = (f32[2,4,2,128,128]{4,3,0,2,1:T(8,128)}, f32[2,4,2,128,128]{4,3,0,2,1:T(8,128)}, u32[]{:S(2)}, u32[]{:S(2)}) collective-permute-start(f32[2,4,2,128,128]{4,3,0,2,1:T(8,128)} %maximum_select_fusion.3), channel_id=1, source_target_pairs={{0,16},{1,17},{2,18},{3,19},{4,20},{5,21},{6,22},{7,23},{8,24},{9,... | collective-permute-start | bytes 3145736 | tf_op jit(solution)/shard_map/ppermute | solution.py:15
  314.6 2.6 copy-start.36
  314.6 2.6 copy-start.40
  314.7 2.6 copy-start.44
  314.7 2.6 copy-start.48
  314.7 2.5 copy-start.59
  314.7 2.5 copy-start.62
  314.7 2.5 copy-start.20
  314.8 2.5 copy-start.25
  314.8 2.5 copy-start.30
  319.0 17.3 %collective-permute-start.5 = (f32[2,4,2,128,128]{4,3,0,2,1:T(8,128)}, f32[2,4,2,128,128]{4,3,0,2,1:T(8,128)}, u32[]{:S(2)}, u32[]{:S(2)}) collective-permute-start(f32[2,4,2,128,128]{4,3,0,2,1:T(8,128)} %maximum_select_fusion.4), channel_id=1, source_target_pairs={{0,32},{1,33},{2,34},{3,35},{4,36},{5,37},{6,38},{7,39},{8,40},{9,... | collective-permute-start | bytes 3145736 | tf_op jit(solution)/shard_map/ppermute | solution.py:15
  370.3 3.2 copy-start.54
  370.3 3.2 copy-start.57
  370.3 3.2 copy-start.60
  370.3 3.2 copy-start.63
  370.9 2.6 copy-start.37
  370.9 2.6 copy-start.41
  370.9 2.6 copy-start.45
  370.9 2.6 copy-start.49
  371.0 2.5 copy-start.70
  371.0 2.5 copy-start.72
  371.0 2.5 copy-start.21
  371.0 2.5 copy-start.26
  371.0 2.5 copy-start.31
  375.2 19.0 %collective-permute-start.6 = (f32[2,4,2,128,128]{4,3,0,2,1:T(8,128)}, f32[2,4,2,128,128]{4,3,0,2,1:T(8,128)}, u32[]{:S(2)}, u32[]{:S(2)}) collective-permute-start(f32[2,4,2,128,128]{4,3,0,2,1:T(8,128)} %maximum_select_fusion.5), channel_id=1, source_target_pairs={{0,64},{1,65},{2,66},{3,67},{4,68},{5,69},{6,70},{7,71},{8,72},{9,... | collective-permute-start | bytes 3145736 | tf_op jit(solution)/shard_map/ppermute | solution.py:15
  427.3 4.1 copy-start.73
  427.9 3.5 copy-start.67
  427.9 3.5 copy-start.69
  427.9 3.5 copy-start.71
  428.4 3.0 copy-start.55
  428.5 3.0 copy-start.58
  428.5 3.0 copy-start.61
  428.5 3.0 copy-start.64
  429.0 2.4 copy-start.38
  429.0 2.4 copy-start.42
  429.1 2.4 copy-start.46
  429.1 2.4 copy-start.50
  434.7 170.4 %copy-start.65 = (f32[2,2,128,128]{3,2,1,0:T(8,128)S(1)}, f32[2,2,128,128]{3,2,1,0:T(8,128)}, u32[]{:S(2)}) copy-start(f32[2,2,128,128]{3,2,1,0:T(8,128)} %param.3) | copy-start | bytes 786436
  434.7 174.1 %collective-permute-start.7 = (f32[2,4,2,128,128]{4,3,0,2,1:T(8,128)S(1)}, f32[2,4,2,128,128]{4,3,0,2,1:T(8,128)}, u32[]{:S(2)}, u32[]{:S(2)}) collective-permute-start(f32[2,4,2,128,128]{4,3,0,2,1:T(8,128)S(1)} %copy-done.74), channel_id=1, source_target_pairs={{0,1},{1,2},{2,3},{3,4},{4,5},{5,6},{6,7},{7,8},{8,9},{9,10},{10,1... | collective-permute-start | bytes 3145736 | tf_op jit(solution)/shard_map/ppermute | solution.py:15
  (37 other events, 55.6 us)
Sparse Core Ops, SparseCore 0:
  433.6 170.3 all-reduce.2
where the time goes:
time: 665 us; the launch traced here: 655 us
  matrix products  264 us (40%)
  waiting for transfers between devices  246 us (37%)
  starting transfers between devices  61.3 us (9%)
  other arithmetic  36.3 us (5%)
  local copies, waits for them, and re-layouts  23.7 us (4%)
  between operations  23.1 us (3%)
    psum x1, waiting for transfers between devices, broadcast(): return lax.psum(kept, axis)  147 us
    ppermute x8, waiting for transfers between devices, shifted(): return lax.ppermute(block, axis, route)  99 us
    dot_general x234, matrix products, complex_product(): jnp.einsum('...ij,...jk->...ik', former_im, latter_re, precision=precise)  72.8 us
    dot_general x234, matrix products, complex_product(): jnp.einsum('...ij,...jk->...ik', former_re, latter_im, precision=precise)  65 us
    dot_general x234, matrix products, complex_product(): jnp.einsum('...ij,...jk->...ik', former_im, latter_im, precision=precise)  63.2 us
    dot_general x234, matrix products, complex_product(): jnp.einsum('...ij,...jk->...ik', former_re, latter_re, precision=precise)  63.2 us
    ppermute x8, starting transfers between devices, shifted(): return lax.ppermute(block, axis, route)  61.3 us
  transfers between devices with their start and end apart: 9, of which 8 were waited for; matrix products, arithmetic and copies ran while one was open for 2% of the time, Pallas kernels for 0%

commit v1 on v0

v1 whole, which is shorter than its diff:
```python
import functools

import jax
import jax.numpy as jnp
from jax import lax
from jax.experimental import pallas as pl
from jax.experimental.pallas import tpu as pltpu
from jax.sharding import PartitionSpec as P

F32 = jnp.float32
BF16 = jnp.bfloat16
N = 128


def split(x):
    high = x.astype(BF16)
    return high, (x - high.astype(F32)).astype(BF16)


def stack(*rows):
    return jnp.concatenate(rows, axis=0)


def square(x):
    turned = jnp.concatenate([-x[:, N:], x[:, :N]], axis=1)
    return jnp.concatenate([x, turned], axis=0)


def dot(a, b):
    return lax.dot(a, b, preferred_element_type=F32)


def times1(rows, matrix):
    return dot(rows.astype(BF16), square(matrix.astype(BF16)))


def times3(rows, matrix):
    rows_high, rows_low = rows if isinstance(rows, tuple) else split(rows)
    high, low = matrix if isinstance(matrix, tuple) else split(matrix)
    wide = square(high)
    return dot(rows_high, wide) + dot(rows_low, wide) + dot(rows_high, square(low))


def unit():
    shape = (N, 2 * N)
    row = lax.broadcasted_iota(jnp.int32, shape, 0)
    column = lax.broadcasted_iota(jnp.int32, shape, 1)
    return (row == column).astype(F32)


def series(bounce, one):
    total = one + bounce
    power = bounce.astype(BF16)
    power = dot(power, square(power)).astype(BF16)
    for step in range(7):
        if step < 6:
            both = dot(stack(total.astype(BF16), power), square(power))
            total = total + both[:N]
            power = both[N:].astype(BF16)
        else:
            total = total + dot(total.astype(BF16), square(power))
    return total


def star(first, second):
    a11, a12, a21, a22 = first
    b11, b12, b21, b22 = second
    one = unit()
    left = split(stack(b11, b21))
    by_right = times3(left, a22)
    bounce, tail = by_right[:N], by_right[N:]
    by_fore = times3(left, a21)
    total = series(bounce, one)
    bounce = split(bounce)
    residual = (one - total) + times3(bounce, total)
    total = total + times1(total, residual)
    lead = split(stack(a12, tail))
    rows = (stack(bounce[0], lead[0]), stack(bounce[1], lead[1]))
    solved = times3(rows, total)
    residual = (one - total) + solved[:N]
    solved = solved[N:] + times1(solved[N:], residual)
    solved = split(solved)
    near = times3(solved, by_fore[:N])
    far = times3(solved, b12)
    return (
        a11 + near[:N],
        far[:N],
        by_fore[N:] + near[N:],
        b22 + far[N:],
    )


def load(ref, *index):
    return jnp.concatenate([ref[index + (0,)], ref[index + (1,)]], axis=1)


def store(ref, index, value):
    ref[index + (0,)] = value[:, :N]
    ref[index + (1,)] = value[:, N:]


def bit(level):
    return (lax.axis_index("chain") >> level) & 1


def mirrored(position, flag):
    return position + flag * (3 - 2 * position)


def first_kernel(sections, received, total, prefix):
    core = bit(0)
    later = bit(0) ^ bit(1)
    own = [load(sections, 0, core, mirrored(p, core)) for p in range(4)]
    other = [load(received, mirrored(p, core)) for p in range(4)]
    result = star(own, other)
    for p in range(4):
        store(total, (mirrored(p, later),), result[p])
        store(prefix, (1, mirrored(p, core)), result[p])

    @pl.when(core == 0)
    def _():
        prefix[0] = sections[0, 0]

    @pl.when(core == 1)
    def _():
        prefix[0] = received[...]


def total_kernel(level, own, received, total):
    flag = bit(level) ^ bit(level + 1)
    result = star([load(own, p) for p in range(4)], [load(received, 3 - p) for p in range(4)])
    for p in range(4):
        store(total, (mirrored(p, flag),), result[p])


def last_kernel(level, own, received, whole):
    flag = bit(level)
    result = star([load(own, p) for p in range(4)], [load(received, 3 - p) for p in range(4)])
    upper = flag == 1
    store(whole, (0,), jnp.where(upper, result[3], result[0]))
    store(whole, (1,), jnp.where(upper, result[1], result[2]))


def prefix_kernel(level, before, prefix, extended):
    flag = bit(level)

    @pl.when(flag == 1)
    def _():
        first = [load(before, p) for p in range(4)]
        for k in range(2):
            result = star(first, [load(prefix, k, p) for p in range(4)])
            for p in range(4):
                store(extended, (k, p), result[p])

    @pl.when(flag == 0)
    def _():
        extended[...] = prefix[...]


def part_kernel(level, keep, before, prefix, extended):
    flag = bit(level)
    core = bit(0)
    which = core if keep else 1 - core

    @pl.when(flag == 1)
    def _():
        first = [load(before, p) for p in range(4)]
        result = star(first, [load(prefix, which, p) for p in range(4)])
        for p in range(4):
            store(extended, (p,), result[p])

    @pl.when(flag == 0)
    def _():
        extended[...] = prefix[which]


def final_kernel(kept, received, whole, other, probes, prefixes, reflected, transmitted):
    core = bit(0)
    prefixes[0, core] = kept[...]
    prefixes[0, 1 - core] = received[...]
    for source, frequency in ((whole, core), (other, 1 - core)):
        rows = stack(load(source, 0), load(source, 1))
        result = times3(rows, load(probes, frequency))
        store(reflected, (frequency,), result[:N])
        store(transmitted, (frequency,), result[N:])


STAR_FLOPS = 2 * 256 * 256 * 128 * 60


def call(kernel, outs, *operands, stars=1):
    in_vmem = pl.BlockSpec(memory_space=pltpu.VMEM)
    shapes = [jax.ShapeDtypeStruct(shape, F32) for shape in outs]
    return pl.pallas_call(
        kernel,
        out_shape=shapes,
        in_specs=[in_vmem] * len(operands),
        out_specs=[in_vmem] * len(outs),
        compiler_params=pltpu.CompilerParams(vmem_limit_bytes=40 << 20),
        cost_estimate=pl.CostEstimate(
            flops=int(STAR_FLOPS * stars), bytes_accessed=2 << 20, transcendentals=0
        ),
    )(*operands)


def exchange(value, mask):
    count = lax.axis_size("chain")
    return lax.ppermute(value, "chain", [(i, i ^ mask) for i in range(count)])


MASKS = (1, 2, 6, 8, 24, 32, 96)
ONE = (4, 2, N, N)
TWO = (2, 4, 2, N, N)


def local(sections, probes):
    core = lax.axis_index("chain") & 1
    sent = lax.dynamic_index_in_dim(sections[0], 1 - core, 0, keepdims=False)
    received = exchange(sent, 1)
    total, prefix = call(first_kernel, [ONE, TWO], sections, received)
    for level in range(1, 6):
        received = exchange(total, MASKS[level])
        (total,) = call(functools.partial(total_kernel, level), [ONE], total, received)
        (prefix,) = call(
            functools.partial(prefix_kernel, level), [TWO], received, prefix, stars=2
        )
    received = exchange(total, MASKS[6])
    (whole,) = call(functools.partial(last_kernel, 6), [(2, 2, N, N)], total, received)
    other = exchange(whole, 1)
    (leaving,) = call(functools.partial(part_kernel, 6, False), [ONE], received, prefix)
    arrived = exchange(leaving, 1)
    (kept,) = call(functools.partial(part_kernel, 6, True), [ONE], received, prefix)
    return tuple(
        call(
            final_kernel,
            [(1,) + TWO, probes.shape, probes.shape],
            kept,
            arrived,
            whole,
            other,
            probes,
        )
    )


def solution(mesh):
    placed = (P("chain", None, None, None, None, None), P(None, None, None, "chain"))
    return jax.shard_map(
        local,
        mesh=mesh,
        in_specs=placed,
        out_specs=(placed[0], placed[1], placed[1]),
        check_vma=False,
    )
```

time: 665 us -> 120 us (0.18)
  the two profiles are of different devices: /device:TPU:1 before, /device:TPU:127 now
where the time goes in v1:
time: 120 us
  Pallas kernels  60.2 us (50%)
  waiting for transfers between devices  49.7 us (41%)
  starting transfers between devices  7.67 us (6%)
    pallas_call x15, Pallas kernels, call(): pl.pallas_call(kernel, out_shape=shapes, in_specs=[in_vmem] * len(operand...  60.2 us
    ppermute x9, waiting for transfers between devices, exchange(): return lax.ppermute(value, 'chain', [(i, i ^ mask) for i in range(count)])  49.7 us
    ppermute x9, starting transfers between devices, exchange(): return lax.ppermute(value, 'chain', [(i, i ^ mask) for i in range(count)])  7.67 us
  transfers between devices with their start and end apart: 9, of which 5 were waited for; matrix products, arithmetic and copies ran while one was open for 0% of the time, Pallas kernels for 31%

profile of v1, /device:TPU:127, one launch (start us, length us, event | category | flops | bytes accessed | tf_op | source)
XLA Modules:
  0.0 119.5 jit_solution(8232787173324653675)
XLA Ops:
  0.6 0.0 copy-start
  0.6 1.2 dynamic-slice_bitcast_fusion
  1.8 0.8 collective-permute-start
  2.6 1.5 %collective-permute-done.received = f32[4,2,128,128]{3,2,1,0:T(8,128)S(1)} collective-permute-done((f32[4,2,128,128]{3,2,1,0:T(8,128)S(1)}, f32[4,2,128,128]{3,2,1,0:T(8,128)S(1)}, u32[]{:S(2)}, u32[]{:S(2)}) %collective-permute-start) | collective-permute-done | bytes 524320 | tf_op jit(solution)/shard_map/ppermute | solution.py:208
  4.1 0.0 copy-done
  4.1 3.2 %shard_map.49 = (f32[4,2,128,128]{3,2,1,0:T(8,128)S(1)}, f32[2,4,2,128,128]{4,3,2,1,0:T(8,128)S(1)}) custom-call(f32[1,2,4,2,128,128]{5,4,3,2,1,0:T(8,128)S(1)} %copy-done, f32[4,2,128,128]{3,2,1,0:T(8,128)S(1)} %collective-permute-done.received), custom_call_target="tpu_custom_call" | custom-call | flops 1006632960 | bytes 2097152 | tf_op jit(solution)/shard_map/pallas_call | solution.py:194
  7.3 0.6 collective-permute-start.1
  7.9 12.6 %collective-permute-done.1.received.before = f32[4,2,128,128]{3,2,1,0:T(8,128)S(1)} collective-permute-done((f32[4,2,128,128]{3,2,1,0:T(8,128)S(1)}, f32[4,2,128,128]{3,2,1,0:T(8,128)S(1)}, u32[]{:S(2)}, u32[]{:S(2)}) %collective-permute-start.1) | collective-permute-done | bytes 524320 | tf_op jit(solution)/shard_map/ppermute | solution.py:208
  20.5 3.1 %shard_map.50.own = f32[4,2,128,128]{3,2,1,0:T(8,128)S(1)} custom-call(f32[4,2,128,128]{3,2,1,0:T(8,128)S(1)} %get-tuple-element.5.own, f32[4,2,128,128]{3,2,1,0:T(8,128)S(1)} %collective-permute-done.1.received.before), custom_call_target="tpu_custom_call" | custom-call | flops 1006632960 | bytes 2097152 | tf_op jit(solution)/shard_map/pallas_call | solution.py:194
  23.6 0.3 collective-permute-start.2
  23.9 13.2 %collective-permute-done.2.received.before = f32[4,2,128,128]{3,2,1,0:T(8,128)S(1)} collective-permute-done((f32[4,2,128,128]{3,2,1,0:T(8,128)S(1)}, f32[4,2,128,128]{3,2,1,0:T(8,128)S(1)}, u32[]{:S(2)}, u32[]{:S(2)}) %collective-permute-start.2) | collective-permute-done | bytes 524320 | tf_op jit(solution)/shard_map/ppermute | solution.py:208
  37.1 3.1 %shard_map.51.own = f32[4,2,128,128]{3,2,1,0:T(8,128)S(1)} custom-call(f32[4,2,128,128]{3,2,1,0:T(8,128)S(1)} %shard_map.50.own, f32[4,2,128,128]{3,2,1,0:T(8,128)S(1)} %collective-permute-done.2.received.before), custom_call_target="tpu_custom_call" | custom-call | flops 1006632960 | bytes 2097152 | tf_op jit(solution)/shard_map/pallas_call | solution.py:194
  40.3 0.5 collective-permute-start.3
  40.8 10.8 %collective-permute-done.3.received.before = f32[4,2,128,128]{3,2,1,0:T(8,128)S(1)} collective-permute-done((f32[4,2,128,128]{3,2,1,0:T(8,128)S(1)}, f32[4,2,128,128]{3,2,1,0:T(8,128)S(1)}, u32[]{:S(2)}, u32[]{:S(2)}) %collective-permute-start.3) | collective-permute-done | bytes 524320 | tf_op jit(solution)/shard_map/ppermute | solution.py:208
  51.6 3.1 %shard_map.52.own = f32[4,2,128,128]{3,2,1,0:T(8,128)S(1)} custom-call(f32[4,2,128,128]{3,2,1,0:T(8,128)S(1)} %shard_map.51.own, f32[4,2,128,128]{3,2,1,0:T(8,128)S(1)} %collective-permute-done.3.received.before), custom_call_target="tpu_custom_call" | custom-call | flops 1006632960 | bytes 2097152 | tf_op jit(solution)/shard_map/pallas_call | solution.py:194
  54.8 0.1 collective-permute-start.4
  54.9 11.5 %collective-permute-done.4.received.before = f32[4,2,128,128]{3,2,1,0:T(8,128)S(1)} collective-permute-done((f32[4,2,128,128]{3,2,1,0:T(8,128)S(1)}, f32[4,2,128,128]{3,2,1,0:T(8,128)S(1)}, u32[]{:S(2)}, u32[]{:S(2)}) %collective-permute-start.4) | collective-permute-done | bytes 524320 | tf_op jit(solution)/shard_map/ppermute | solution.py:208
  66.4 3.1 %shard_map.53.own = f32[4,2,128,128]{3,2,1,0:T(8,128)S(1)} custom-call(f32[4,2,128,128]{3,2,1,0:T(8,128)S(1)} %shard_map.52.own, f32[4,2,128,128]{3,2,1,0:T(8,128)S(1)} %collective-permute-done.4.received.before), custom_call_target="tpu_custom_call" | custom-call | flops 1006632960 | bytes 2097152 | tf_op jit(solution)/shard_map/pallas_call | solution.py:194
  69.5 0.2 collective-permute-start.5
  69.8 6.1 %shard_map.55.prefix = f32[2,4,2,128,128]{4,3,2,1,0:T(8,128)S(1)} custom-call(f32[4,2,128,128]{3,2,1,0:T(8,128)S(1)} %collective-permute-done.1.received.before, f32[2,4,2,128,128]{4,3,2,1,0:T(8,128)S(1)} %get-tuple-element.6.prefix), custom_call_target="tpu_custom_call" | custom-call | flops 2013265920 | bytes 2097152 | tf_op jit(solution)/shard_map/pallas_call | solution.py:194
  75.9 6.0 %shard_map.56.prefix = f32[2,4,2,128,128]{4,3,2,1,0:T(8,128)S(1)} custom-call(f32[4,2,128,128]{3,2,1,0:T(8,128)S(1)} %collective-permute-done.2.received.before, f32[2,4,2,128,128]{4,3,2,1,0:T(8,128)S(1)} %shard_map.55.prefix), custom_call_target="tpu_custom_call" | custom-call | flops 2013265920 | bytes 2097152 | tf_op jit(solution)/shard_map/pallas_call | solution.py:194
  81.9 0.0 collective-permute-done.5.received.before
  81.9 3.1 %shard_map.54.own = f32[4,2,128,128]{3,2,1,0:T(8,128)S(1)} custom-call(f32[4,2,128,128]{3,2,1,0:T(8,128)S(1)} %shard_map.53.own, f32[4,2,128,128]{3,2,1,0:T(8,128)S(1)} %collective-permute-done.5.received.before), custom_call_target="tpu_custom_call" | custom-call | flops 1006632960 | bytes 2097152 | tf_op jit(solution)/shard_map/pallas_call | solution.py:194
  85.1 0.4 collective-permute-start.6
  85.5 6.0 %shard_map.57.prefix = f32[2,4,2,128,128]{4,3,2,1,0:T(8,128)S(1)} custom-call(f32[4,2,128,128]{3,2,1,0:T(8,128)S(1)} %collective-permute-done.3.received.before, f32[2,4,2,128,128]{4,3,2,1,0:T(8,128)S(1)} %shard_map.56.prefix), custom_call_target="tpu_custom_call" | custom-call | flops 2013265920 | bytes 2097152 | tf_op jit(solution)/shard_map/pallas_call | solution.py:194
  91.5 6.3 %shard_map.58.prefix = f32[2,4,2,128,128]{4,3,2,1,0:T(8,128)S(1)} custom-call(f32[4,2,128,128]{3,2,1,0:T(8,128)S(1)} %collective-permute-done.4.received.before, f32[2,4,2,128,128]{4,3,2,1,0:T(8,128)S(1)} %shard_map.57.prefix), custom_call_target="tpu_custom_call" | custom-call | flops 2013265920 | bytes 2097152 | tf_op jit(solution)/shard_map/pallas_call | solution.py:194
  97.8 6.0 %shard_map.59.prefix = f32[2,4,2,128,128]{4,3,2,1,0:T(8,128)S(1)} custom-call(f32[4,2,128,128]{3,2,1,0:T(8,128)S(1)} %collective-permute-done.5.received.before, f32[2,4,2,128,128]{4,3,2,1,0:T(8,128)S(1)} %shard_map.58.prefix), custom_call_target="tpu_custom_call" | custom-call | flops 2013265920 | bytes 2097152 | tf_op jit(solution)/shard_map/pallas_call | solution.py:194
  103.9 0.0 collective-permute-done.6.before.received
  103.9 3.1 %shard_map.61 = f32[4,2,128,128]{3,2,1,0:T(8,128)S(1)} custom-call(f32[4,2,128,128]{3,2,1,0:T(8,128)S(1)} %collective-permute-done.6.before.received, f32[2,4,2,128,128]{4,3,2,1,0:T(8,128)S(1)} %shard_map.59.prefix), custom_call_target="tpu_custom_call" | custom-call | flops 1006632960 | bytes 2097152 | tf_op jit(solution)/shard_map/pallas_call | solution.py:194
  107.0 4.6 %collective-permute-start.7 = (f32[4,2,128,128]{3,2,1,0:T(8,128)S(1)}, f32[4,2,128,128]{3,2,1,0:T(8,128)S(1)}, u32[]{:S(2)}, u32[]{:S(2)}) collective-permute-start(f32[4,2,128,128]{3,2,1,0:T(8,128)S(1)} %shard_map.61), channel_id=1, source_target_pairs={{0,1},{1,0},{2,3},{3,2},{4,5},{5,4},{6,7},{7,6},{8,9},{9,8},{10,11... | collective-permute-start | bytes 1572872 | tf_op jit(solution)/shard_map/ppermute | solution.py:208
  111.6 3.1 %shard_map.62.whole = f32[2,2,128,128]{3,2,1,0:T(8,128)S(1)} custom-call(f32[4,2,128,128]{3,2,1,0:T(8,128)S(1)} %shard_map.54.own, f32[4,2,128,128]{3,2,1,0:T(8,128)S(1)} %collective-permute-done.6.before.received), custom_call_target="tpu_custom_call" | custom-call | flops 1006632960 | bytes 2097152 | tf_op jit(solution)/shard_map/pallas_call | solution.py:194
  114.8 0.0 copy-start.1
  114.8 0.1 collective-permute-start.8
  114.9 3.1 %shard_map.60.kept = f32[4,2,128,128]{3,2,1,0:T(8,128)S(1)} custom-call(f32[4,2,128,128]{3,2,1,0:T(8,128)S(1)} %collective-permute-done.6.before.received, f32[2,4,2,128,128]{4,3,2,1,0:T(8,128)S(1)} %shard_map.59.prefix), custom_call_target="tpu_custom_call" | custom-call | flops 1006632960 | bytes 2097152 | tf_op jit(solution)/shard_map/pallas_call | solution.py:194
  118.0 0.0 collective-permute-done.8.other
  118.0 0.0 collective-permute-done.7.received
  118.0 0.0 copy-done.1
  118.0 1.5 %shard_map.63 = (f32[1,2,4,2,128,128]{5,4,3,2,1,0:T(8,128)}, f32[2,2,128,128]{3,2,1,0:T(8,128)}, f32[2,2,128,128]{3,2,1,0:T(8,128)}) custom-call(f32[4,2,128,128]{3,2,1,0:T(8,128)S(1)} %shard_map.60.kept, f32[4,2,128,128]{3,2,1,0:T(8,128)S(1)} %collective-permute-done.7.received, f32[2,2,128,128]{3,2,1,0:T(8,128)S(1)} %shard_map.62.whole, ...), custom_call_target="tpu_custom_call" | custom-call | flops 1006632960 | bytes 2097152 | tf_op jit(solution)/shard_map/pallas_call | solution.py:194
Async XLA Ops:
  0.6 3.5 %copy-start = (f32[1,2,4,2,128,128]{5,4,3,2,1,0:T(8,128)S(1)}, f32[1,2,4,2,128,128]{5,4,3,2,1,0:T(8,128)}, u32[]{:S(2)}) copy-start(f32[1,2,4,2,128,128]{5,4,3,2,1,0:T(8,128)} %sections.1) | copy-start | bytes 3145732
  1.8 2.3 %collective-permute-start = (f32[4,2,128,128]{3,2,1,0:T(8,128)S(1)}, f32[4,2,128,128]{3,2,1,0:T(8,128)S(1)}, u32[]{:S(2)}, u32[]{:S(2)}) collective-permute-start(f32[4,2,128,128]{3,2,1,0:T(8,128)S(1)} %dynamic-slice_bitcast_fusion), channel_id=1, source_target_pairs={{0,1},{1,0},{2,3},{3,2},{4,5},{5,4},{6,7},{7,6},{8,9},{9,8},{10,11... | collective-permute-start | bytes 1572872 | tf_op jit(solution)/shard_map/ppermute | solution.py:208
  7.3 13.2 %collective-permute-start.1 = (f32[4,2,128,128]{3,2,1,0:T(8,128)S(1)}, f32[4,2,128,128]{3,2,1,0:T(8,128)S(1)}, u32[]{:S(2)}, u32[]{:S(2)}) collective-permute-start(f32[4,2,128,128]{3,2,1,0:T(8,128)S(1)} %get-tuple-element.5.own), channel_id=1, source_target_pairs={{0,2},{1,3},{2,0},{3,1},{4,6},{5,7},{6,4},{7,5},{8,10},{9,11},{10,... | collective-permute-start | bytes 1572872 | tf_op jit(solution)/shard_map/ppermute | solution.py:208
  23.6 13.5 %collective-permute-start.2 = (f32[4,2,128,128]{3,2,1,0:T(8,128)S(1)}, f32[4,2,128,128]{3,2,1,0:T(8,128)S(1)}, u32[]{:S(2)}, u32[]{:S(2)}) collective-permute-start(f32[4,2,128,128]{3,2,1,0:T(8,128)S(1)} %shard_map.50.own), channel_id=1, source_target_pairs={{0,6},{1,7},{2,4},{3,5},{4,2},{5,3},{6,0},{7,1},{8,14},{9,15},{10,... | collective-permute-start | bytes 1572872 | tf_op jit(solution)/shard_map/ppermute | solution.py:208
  40.3 11.4 %collective-permute-start.3 = (f32[4,2,128,128]{3,2,1,0:T(8,128)S(1)}, f32[4,2,128,128]{3,2,1,0:T(8,128)S(1)}, u32[]{:S(2)}, u32[]{:S(2)}) collective-permute-start(f32[4,2,128,128]{3,2,1,0:T(8,128)S(1)} %shard_map.51.own), channel_id=1, source_target_pairs={{0,8},{1,9},{2,10},{3,11},{4,12},{5,13},{6,14},{7,15},{8,0},{9,1},... | collective-permute-start | bytes 1572872 | tf_op jit(solution)/shard_map/ppermute | solution.py:208
  54.8 11.6 %collective-permute-start.4 = (f32[4,2,128,128]{3,2,1,0:T(8,128)S(1)}, f32[4,2,128,128]{3,2,1,0:T(8,128)S(1)}, u32[]{:S(2)}, u32[]{:S(2)}) collective-permute-start(f32[4,2,128,128]{3,2,1,0:T(8,128)S(1)} %shard_map.52.own), channel_id=1, source_target_pairs={{0,24},{1,25},{2,26},{3,27},{4,28},{5,29},{6,30},{7,31},{8,16},{9,... | collective-permute-start | bytes 1572872 | tf_op jit(solution)/shard_map/ppermute | solution.py:208
  69.5 12.4 %collective-permute-start.5 = (f32[4,2,128,128]{3,2,1,0:T(8,128)S(1)}, f32[4,2,128,128]{3,2,1,0:T(8,128)S(1)}, u32[]{:S(2)}, u32[]{:S(2)}) collective-permute-start(f32[4,2,128,128]{3,2,1,0:T(8,128)S(1)} %shard_map.53.own), channel_id=1, source_target_pairs={{0,32},{1,33},{2,34},{3,35},{4,36},{5,37},{6,38},{7,39},{8,40},{9,... | collective-permute-start | bytes 1572872 | tf_op jit(solution)/shard_map/ppermute | solution.py:208
  85.1 18.8 %collective-permute-start.6 = (f32[4,2,128,128]{3,2,1,0:T(8,128)S(1)}, f32[4,2,128,128]{3,2,1,0:T(8,128)S(1)}, u32[]{:S(2)}, u32[]{:S(2)}) collective-permute-start(f32[4,2,128,128]{3,2,1,0:T(8,128)S(1)} %shard_map.54.own), channel_id=1, source_target_pairs={{0,96},{1,97},{2,98},{3,99},{4,100},{5,101},{6,102},{7,103},{8,104... | collective-permute-start | bytes 1572872 | tf_op jit(solution)/shard_map/ppermute | solution.py:208
  107.0 11.0 %collective-permute-start.7 = (f32[4,2,128,128]{3,2,1,0:T(8,128)S(1)}, f32[4,2,128,128]{3,2,1,0:T(8,128)S(1)}, u32[]{:S(2)}, u32[]{:S(2)}) collective-permute-start(f32[4,2,128,128]{3,2,1,0:T(8,128)S(1)} %shard_map.61), channel_id=1, source_target_pairs={{0,1},{1,0},{2,3},{3,2},{4,5},{5,4},{6,7},{7,6},{8,9},{9,8},{10,11... | collective-permute-start | bytes 1572872 | tf_op jit(solution)/shard_map/ppermute | solution.py:208
  114.8 3.3 %copy-start.1 = (f32[2,2,128,128]{3,2,1,0:T(8,128)S(1)}, f32[2,2,128,128]{3,2,1,0:T(8,128)}, u32[]{:S(2)}) copy-start(f32[2,2,128,128]{3,2,1,0:T(8,128)} %probes.1) | copy-start | bytes 786436
  114.8 3.2 %collective-permute-start.8 = (f32[2,2,128,128]{3,2,1,0:T(8,128)S(1)}, f32[2,2,128,128]{3,2,1,0:T(8,128)S(1)}, u32[]{:S(2)}, u32[]{:S(2)}) collective-permute-start(f32[2,2,128,128]{3,2,1,0:T(8,128)S(1)} %shard_map.62.whole), channel_id=1, source_target_pairs={{0,1},{1,0},{2,3},{3,2},{4,5},{5,4},{6,7},{7,6},{8,9},{9,8},{10,11... | collective-permute-start | bytes 786440 | tf_op jit(solution)/shard_map/ppermute | solution.py:208
